TPU v7x, 32 devices: a whole 2x2x4 slice. The times are simulated.
32 devices in a mesh: samples: 2 (over y), theta: 4 (over z), band: 2 (over x), row: 2 (over core).
Axes of the slice: x: 2, y: 2, z: 4, core: 2. Of those that a mesh axis runs over, the one named last changes fastest.
Arguments:
- adjoint: float32 [4, 5, 64, 32, 128], P(('samples', 'row'), None, 'theta', 'band'), parts along dimension 0, may hold values from -6 to 6
- objective_grad: float32 [4, 5, 64, 32, 128], P(('samples', 'row'), None, 'theta', 'band'), parts along dimension 0, may hold values from -12 to 12
- face_coef: float32 [4, 3, 64, 32, 128], P(('samples', 'row'), None, 'theta', 'band'), parts along dimension 0, may hold values from 0.5 to 2
- source: float32 [4, 64, 32, 128], P(('samples', 'row'), 'theta', 'band'), parts along dimension 0, may hold values from 0.5 to 4
- flux_jac: float32 [2, 3, 2, 5, 5], P('row'), may hold values from -2.5 to 2.5
- mix_weight: float32 [4, 64, 32], P(('samples', 'row'), 'theta', 'band'), parts along dimension 0, may hold values from 0.25 to 1
- mix_map: int32 [4, 32], P(('samples', 'row'), 'band'), parts along dimension 0, may hold values from 0 to 31
- mix_jac: float32 [2, 5, 5], P('row'), may hold values from -2.5 to 2.5
- surf_weight: float32 [4, 5, 4, 32, 128], P(('samples', 'row'), None, 'theta', 'band'), parts along dimension 0, may hold values from -1.5 to 1.5
- patch_mode: int32 [4, 4, 32], P(('samples', 'row'), 'theta', 'band'), parts along dimension 0, may hold values from 0 to 31
Outputs:
- adjoint_out: float32 [4, 5, 64, 32, 128], P(('samples', 'row'), None, 'theta', 'band'), parts along dimension 0
- sensitivity: float32 [64, 128], P(('samples', 'theta', 'band', 'row')), parts along dimension 0
There are 2 independent parts, one for each index of `samples`. A program takes and returns all parts, laid end to end along the dimension named above; an argument that names none is the same for every part. Nothing has to cross between parts.
All inputs are finite; a program needn't handle non-finite values.
Results may differ from a plain program's by a relative error of at most 0.0001.
Values sent between devices are 32-bit elements; how exact they have to be, the bound alone decides.
A program may use at most 64 MiB of HBM per device.

v0:
```python
import jax
import jax.numpy as jnp
from jax import lax
from jax.sharding import PartitionSpec as P

ITERS = 3
MODES_DEV = 2


OMEGA = 0.8


def partner(value, axis, apart):
    return lax.ppermute(value, axis, [(i, i ^ 1 << apart) for i in range(lax.axis_size(axis))])


def from_behind(block, axis, distance):
    devices = range(lax.axis_size(axis))
    route = [((i - distance) % len(devices), i) for i in devices]
    return lax.ppermute(block, axis, route)


def passed_along(block, axis, distance):
    devices = range(lax.axis_size(axis))
    route = [(i - distance, i) for i in devices if i - distance in devices]
    return lax.ppermute(block, axis, route)


def extended(value, sides, width, wrap):
    for axis, dim in sides:
        devices, length = (lax.axis_size(axis), value.shape[dim])
        up = [(i, (i + 1) % devices) for i in range(devices if wrap else devices - 1)]
        down = [(j, i) for i, j in up]
        last = lax.slice_in_dim(value, length - width, length, axis=dim)
        first = lax.slice_in_dim(value, 0, width, axis=dim)
        before = lax.ppermute(last, axis, up)
        after = lax.ppermute(first, axis, down)
        value = jnp.concatenate([before, value, after], axis=dim)
    return value


def lower_shift(values, axis):
    zero_layer = jnp.zeros_like(lax.slice_in_dim(values, 0, 1, axis=axis))
    return jnp.concatenate(
        [zero_layer, lax.slice_in_dim(values, 0, values.shape[axis] - 1, axis=axis)], axis
    )


def upper_shift(values, axis):
    zero_layer = jnp.zeros_like(lax.slice_in_dim(values, 0, 1, axis=axis))
    return jnp.concatenate(
        [lax.slice_in_dim(values, 1, values.shape[axis], axis=axis), zero_layer], axis
    )


def apply_block(matrix, values):
    return jnp.einsum("gf,gtra->ftra", matrix, values, precision=lax.Precision.HIGHEST)


def transposed_flux(center, uppers, lowers, coef_up, coef_low, jacobian):
    total = jnp.zeros_like(center)
    for direction in range(3):
        total = total + apply_block(
            jacobian[direction, 0], coef_up[direction][None] * (center - uppers[direction])
        )
        total = total + apply_block(
            jacobian[direction, 1], coef_low[direction][None] * (lowers[direction] - center)
        )
    return total


def local(
    adjoint,
    objective_grad,
    face_coef,
    source,
    flux_jac,
    mix_weight,
    mix_map,
    mix_jac,
    surf_weight,
    patch_mode,
):
    fields_now = adjoint[0]
    grad_local = objective_grad[0]
    coef_local = face_coef[0]
    source_local = source[0]
    jacobian = flux_jac[0]
    weights_local = mix_weight[0]
    map_local = mix_map[0]
    mix_matrix = mix_jac[0]
    n_rad_cells = fields_now.shape[2]
    n_axial = fields_now.shape[3]
    band_count = lax.axis_size("band")
    n_radial = n_rad_cells * band_count
    row_index = lax.axis_index("row")
    band_index = lax.axis_index("band")
    face_pos = jnp.where(row_index == 0, n_axial - 1, 0)
    axial_sel = (jnp.arange(n_axial) == face_pos).astype(jnp.float32)
    row_onehot = (map_local[:, None] == jnp.arange(n_radial)[None, :]).astype(jnp.float32)
    coef_up = (coef_local[0], coef_local[1], coef_local[2])
    theta_prev = from_behind(coef_local[0][-1:], "theta", 1)
    band_prev = passed_along(coef_local[1][:, -1:], "band", 1)
    coef_low = (
        jnp.concatenate([theta_prev, coef_local[0][:-1]], 0),
        jnp.concatenate([band_prev, coef_local[1][:, :-1]], 1),
        lower_shift(coef_local[2], 2),
    )
    diagonal = source_local
    for direction in range(3):
        diagonal = diagonal + coef_up[direction] + coef_low[direction]
    for step in range(ITERS):
        theta_ext = extended(fields_now, (("theta", 1),), 1, True)
        band_ext = extended(fields_now, (("band", 2),), 1, False)
        uppers = (theta_ext[:, 2:], band_ext[:, :, 2:], upper_shift(fields_now, 3))
        lowers = (theta_ext[:, :-2], band_ext[:, :, :-2], lower_shift(fields_now, 3))
        flux = transposed_flux(fields_now, uppers, lowers, coef_up, coef_low, jacobian)
        face_vals = jnp.sum(fields_now * axial_sel, axis=3)
        face_sum = jnp.sum(face_vals * weights_local[None], axis=1)
        face_sum = lax.psum(face_sum, "theta")
        matched = jnp.dot(face_sum, row_onehot, precision=lax.Precision.HIGHEST)
        matched = lax.psum(matched, "band")
        other_row = partner(matched, "row", 0)
        plane = jnp.einsum("gf,gr->fr", mix_matrix, other_row, precision=lax.Precision.HIGHEST)
        plane_own = lax.dynamic_slice_in_dim(plane, band_index * n_rad_cells, n_rad_cells, 1)
        resid = flux + plane_own[:, None, :, None] * axial_sel - grad_local
        fields_now = fields_now - OMEGA * resid / diagonal
    surface = fields_now[:, 0]
    weighted = jnp.sum(surf_weight[0, :, 0] * surface, axis=0)
    modes_local = patch_mode[0, 0]
    select = (
        modes_local[None, :]
        == jnp.arange(MODES_DEV * lax.axis_size(("theta", "band", "row")))[:, None]
    ).astype(jnp.float32)
    sensitivity = lax.psum_scatter(
        jnp.dot(select, weighted, precision=lax.Precision.HIGHEST),
        ("theta", "band", "row"),
        scatter_dimension=0,
        tiled=True,
    )
    return (fields_now[None], sensitivity)


def solution(mesh):
    placed = (
        P(("samples", "row"), None, "theta", "band", None),
        P(("samples", "row"), None, "theta", "band", None),
        P(("samples", "row"), None, "theta", "band", None),
        P(("samples", "row"), "theta", "band", None),
        P("row", None, None, None, None),
        P(("samples", "row"), "theta", "band"),
        P(("samples", "row"), "band"),
        P("row", None, None),
        P(("samples", "row"), None, "theta", "band", None),
        P(("samples", "row"), "theta", "band"),
    )
    return jax.shard_map(
        local,
        mesh=mesh,
        in_specs=placed,
        out_specs=(
            P(("samples", "row"), None, "theta", "band", None),
            P(("samples", "theta", "band", "row"), None),
        ),
        check_vma=False,
    )
```

profile of v0, /device:TPU:0, one launch (start us, length us, event | category | flops | bytes accessed | tf_op | source)
XLA Modules:
  0.0 177.4 jit_solution(11073530076337096669)
XLA Ops:
  0.6 0.8 slice_bitcast_fusion.5
  1.4 3.0 %collective-permute-start.1 = (f32[1,16,128]{2,1,0:T(8,128)S(1)}, f32[1,16,128]{2,1,0:T(8,128)S(1)}, u32[]{:S(2)}, u32[]{:S(2)}) collective-permute-start(f32[1,16,128]{2,1,0:T(8,128)S(1)} %slice_bitcast_fusion.5), channel_id=1, source_target_pairs={{12,0},{0,4},{4,8},{8,12},{13,1},{1,5},{5,9},{9,13},{14,2},{2,6},{... | collective-permute-start | bytes 24584 | tf_op jit(solution)/shard_map/ppermute | solution.py:20
  4.4 1.1 slice_bitcast_fusion
  5.5 3.4 %collective-permute-start.4 = (f32[16,1,128]{2,1,0:T(1,128)S(1)}, f32[16,1,128]{2,1,0:T(1,128)S(1)}, u32[]{:S(2)}, u32[]{:S(2)}) collective-permute-start(f32[16,1,128]{2,1,0:T(1,128)S(1)} %slice.228), channel_id=1, source_target_pairs={{0,2},{1,3},{4,6},{5,7},{8,10},{9,11},{12,14},{13,15},{16,18},{17,... | collective-permute-start | bytes 24584 | tf_op jit(solution)/shard_map/ppermute | solution.py:26
  9.7 10.8 %psum.42 = f32[5,16]{0,1:T(8,128)S(1)} all-reduce(f32[5,16]{0,1:T(8,128)S(1)} %multiply_reduce_fusion.5), channel_id=1, replica_groups=mesh['samples'=2,'theta'=4,'band'=2,'row'=2] {'theta'}, use_global_device_ids=true, to_apply=%region_2.3 | all-reduce | flops 80 | bytes 640 | tf_op jit(solution)/shard_map/psum | solution.py:120
  20.5 0.6 copy-done.19
  21.3 4.9 %psum.43 = f32[5,32]{1,0:T(8,128)S(1)} all-reduce(f32[5,32]{1,0:T(8,128)S(1)} %fusion.116), channel_id=1, replica_groups=mesh['samples'=2,'theta'=4,'band'=2,'row'=2] {'band'}, use_global_device_ids=true, to_apply=%region_3.4 | all-reduce | flops 160 | bytes 1280 | tf_op jit(solution)/shard_map/psum | solution.py:122
  26.8 3.8 %collective-permute-start = (f32[5,1,16,128]{3,0,2,1:T(8,128)S(1)}, f32[5,1,16,128]{3,0,2,1:T(8,128)S(1)}, u32[]{:S(2)}, u32[]{:S(2)}) collective-permute-start(f32[5,1,16,128]{3,0,2,1:T(8,128)S(1)} %get-tuple-element.26), channel_id=1, source_target_pairs={{4,0},{8,4},{12,8},{0,12},{5,1},{9,5},{13,9},{1,13},{6,2},{10,6},{... | collective-permute-start | bytes 122888 | tf_op jit(solution)/shard_map/ppermute | solution.py:37
  30.7 1.7 fusion.153
  33.6 1.3 collective-permute-start.3
  35.4 4.5 %collective-permute-start.5 = (f32[5,16,1,128]{3,0,2,1:T(8,128)S(1)}, f32[5,16,1,128]{3,0,2,1:T(8,128)S(1)}, u32[]{:S(2)}, u32[]{:S(2)}) collective-permute-start(f32[5,16,1,128]{3,0,2,1:T(8,128)S(1)} %get-tuple-element.24), channel_id=1, source_target_pairs={{0,2},{1,3},{4,6},{5,7},{8,10},{9,11},{12,14},{13,15},{16,18},{17,... | collective-permute-start | bytes 122888 | tf_op jit(solution)/shard_map/ppermute | solution.py:36
  40.1 1.1 fusion.62
  41.3 1.1 convolution_add_fusion.14
  42.5 1.1 convolution_add_fusion.13
  43.6 1.1 convolution_add_fusion.12
  44.8 1.5 convolution_add_fusion.11
  46.4 2.6 %multiply_reduce_fusion.1 = (f32[5,16,16]{0,2,1:T(8,128)S(1)}, f32[5,16,16,128]{3,0,2,1:T(8,128)S(1)}) fusion(f32[128]{0:T(128)S(1)} %compare_convert_fusion, f32[16,16,128]{2,1,0:T(8,128)S(1)} %get-tuple-element.8, f32[1,5,16,16,128]{4,3,2,1,0:T(8,128)S(1)} %copy-done.15, f32[5,16,128]{2,0,1:T(8,128)S(1)} %broadcast_multiply_fusion.2, ...), kind=kOutput, calls=%fused_computation.92 | convolution fusion | flops 11467520 | bytes 5056000 | tf_op jit(solution)/shard_map/gf,gtra->ftra/dot_general | solution.py:57
  49.0 1.3 fusion.150
  50.4 8.7 %psum.44 = f32[5,16]{0,1:T(8,128)S(1)} all-reduce(f32[5,16]{0,1:T(8,128)S(1)} %multiply_reduce_fusion.4), channel_id=1, replica_groups=mesh['samples'=2,'theta'=4,'band'=2,'row'=2] {'theta'}, use_global_device_ids=true, to_apply=%region_6.7 | all-reduce | flops 80 | bytes 640 | tf_op jit(solution)/shard_map/psum | solution.py:120
  59.3 4.9 %psum.45 = f32[5,32]{1,0:T(8,128)S(1)} all-reduce(f32[5,32]{1,0:T(8,128)S(1)} %fusion.115), channel_id=1, replica_groups=mesh['samples'=2,'theta'=4,'band'=2,'row'=2] {'band'}, use_global_device_ids=true, to_apply=%region_7.8 | all-reduce | flops 160 | bytes 1280 | tf_op jit(solution)/shard_map/psum | solution.py:122
  64.3 2.0 %collective-permute-start.8 = (f32[5,1,16,128]{3,0,2,1:T(8,128)S(1)}, f32[5,1,16,128]{3,0,2,1:T(8,128)S(1)}, u32[]{:S(2)}, u32[]{:S(2)}) collective-permute-start(f32[5,1,16,128]{3,0,2,1:T(8,128)S(1)} %get-tuple-element.21), channel_id=1, source_target_pairs={{0,4},{4,8},{8,12},{12,0},{1,5},{5,9},{9,13},{13,1},{2,6},{6,10},{... | collective-permute-start | bytes 122888 | tf_op jit(solution)/shard_map/ppermute | solution.py:36
  66.2 1.9 %collective-permute-start.7 = (f32[5,1,16,128]{3,0,2,1:T(8,128)S(1)}, f32[5,1,16,128]{3,0,2,1:T(8,128)S(1)}, u32[]{:S(2)}, u32[]{:S(2)}) collective-permute-start(f32[5,1,16,128]{3,0,2,1:T(8,128)S(1)} %get-tuple-element.20), channel_id=1, source_target_pairs={{4,0},{8,4},{12,8},{0,12},{5,1},{9,5},{13,9},{1,13},{6,2},{10,6},{... | collective-permute-start | bytes 122888 | tf_op jit(solution)/shard_map/ppermute | solution.py:37
  68.2 1.3 collective-permute-start.9
  69.4 4.5 %collective-permute-start.10 = (f32[5,16,1,128]{3,0,2,1:T(8,128)S(1)}, f32[5,16,1,128]{3,0,2,1:T(8,128)S(1)}, u32[]{:S(2)}, u32[]{:S(2)}) collective-permute-start(f32[5,16,1,128]{3,0,2,1:T(8,128)S(1)} %get-tuple-element.18), channel_id=1, source_target_pairs={{0,2},{1,3},{4,6},{5,7},{8,10},{9,11},{12,14},{13,15},{16,18},{17,... | collective-permute-start | bytes 122888 | tf_op jit(solution)/shard_map/ppermute | solution.py:36
  74.5 1.1 fusion.45
  75.6 1.1 convolution_add_fusion.9
  76.8 1.1 convolution_add_fusion.8
  77.9 1.1 convolution_add_fusion.7
  79.1 1.2 convolution_add_fusion.6
  80.6 2.1 %multiply_reduce_fusion = (f32[5,16,16]{0,2,1:T(8,128)S(1)}, f32[5,16,16,128]{3,0,2,1:T(8,128)S(1)}) fusion(f32[128]{0:T(128)S(1)} %compare_convert_fusion, f32[5,16,16,128]{3,0,2,1:T(8,128)S(1)} %get-tuple-element.34, f32[16,16,128]{2,1,0:T(8,128)S(1)} %copy-done.8, f32[1,5,16,16,128]{4,3,2,1,0:T(8,128)S(1)} %copy-done.16, ...), kind=kOutput, calls=%fused_computation.85 | convolution fusion | flops 11467520 | bytes 5842432 | tf_op jit(solution)/shard_map/gf,gtra->ftra/dot_general | solution.py:57
  82.6 0.6 fusion.149
  83.3 1.3 fusion.147
  84.7 8.7 %psum.46 = f32[5,16]{0,1:T(8,128)S(1)} all-reduce(f32[5,16]{0,1:T(8,128)S(1)} %multiply_reduce_fusion.3), channel_id=1, replica_groups=mesh['samples'=2,'theta'=4,'band'=2,'row'=2] {'theta'}, use_global_device_ids=true, to_apply=%region_10.11 | all-reduce | flops 80 | bytes 640 | tf_op jit(solution)/shard_map/psum | solution.py:120
  93.6 4.9 %psum.47 = f32[5,32]{1,0:T(8,128)S(1)} all-reduce(f32[5,32]{1,0:T(8,128)S(1)} %fusion.114), channel_id=1, replica_groups=mesh['samples'=2,'theta'=4,'band'=2,'row'=2] {'band'}, use_global_device_ids=true, to_apply=%region_11.12 | all-reduce | flops 160 | bytes 1280 | tf_op jit(solution)/shard_map/psum | solution.py:122
  98.5 0.6 fusion.148
  99.2 1.7 collective-permute-start.13
  100.9 2.1 %collective-permute-start.12 = (f32[5,1,16,128]{3,0,2,1:T(8,128)S(1)}, f32[5,1,16,128]{3,0,2,1:T(8,128)S(1)}, u32[]{:S(2)}, u32[]{:S(2)}) collective-permute-start(f32[5,1,16,128]{3,0,2,1:T(8,128)S(1)} %get-tuple-element.14), channel_id=1, source_target_pairs={{4,0},{8,4},{12,8},{0,12},{5,1},{9,5},{13,9},{1,13},{6,2},{10,6},{... | collective-permute-start | bytes 122888 | tf_op jit(solution)/shard_map/ppermute | solution.py:37
  103.0 1.3 collective-permute-start.14
  104.3 4.8 %collective-permute-start.15 = (f32[5,16,1,128]{3,0,2,1:T(8,128)S(1)}, f32[5,16,1,128]{3,0,2,1:T(8,128)S(1)}, u32[]{:S(2)}, u32[]{:S(2)}) collective-permute-start(f32[5,16,1,128]{3,0,2,1:T(8,128)S(1)} %get-tuple-element.12), channel_id=1, source_target_pairs={{0,2},{1,3},{4,6},{5,7},{8,10},{9,11},{12,14},{13,15},{16,18},{17,... | collective-permute-start | bytes 122888 | tf_op jit(solution)/shard_map/ppermute | solution.py:36
  109.5 1.1 fusion.28
  110.7 1.1 convolution_add_fusion.4
  111.9 1.1 convolution_add_fusion.3
  113.0 1.1 convolution_add_fusion.2
  114.2 1.1 convolution_add_fusion.1
  115.6 1.9 %fusion.5 = f32[5,16,16,128]{3,0,2,1:T(8,128)S(1)} fusion(f32[5,16,16,128]{3,0,2,1:T(8,128)S(1)} %get-tuple-element.36, f32[16,16,128,5]{2,3,1,0:T(8,128)S(1)} %convolution_add_fusion.1, f32[1,5,16,16,128]{4,3,2,1,0:T(8,128)S(1)} %copy-done.17, f32[5,16,16,127]{3,0,2,1:T(8,128)S(1)} %copy-done.4, f32[5,16,128]{2,0,1:T(8,128)S(1)} %broadcast_multiply_fusion, ...), kind=kOutput, calls=%fused_computation.6 | convolution fusion | flops 11141120 | bytes 5836800 | tf_op jit(solution)/shard_map/gf,gtra->ftra/dot_general | solution.py:57
  117.4 1.0 copy.89
  118.4 0.6 copy-done.14
  119.2 57.6 %all-reduce.7 = f32[32,128]{1,0:T(8,128)S(1)} all-reduce(f32[32,128]{1,0:T(8,128)S(1)} %fusion.112), channel_id=2, replica_groups=mesh['samples'=2,'theta'=4,'band'=2,'row'=2] {'theta','band','row'}, use_global_device_ids=true, to_apply=%region_13.14.clone | all-reduce | flops 4096 | bytes 32768
  (94 shorter events, 5.5 us)
Async XLA Ops:
  0.6 8.3 %copy-start = (f32[1,5,16,16,128]{4,3,2,1,0:T(8,128)S(1)}, f32[1,5,16,16,128]{4,3,2,1,0:T(8,128)}, u32[]{:S(2)}) copy-start(f32[1,5,16,16,128]{4,3,2,1,0:T(8,128)} %param.10) | copy-start | bytes 1966084
  1.4 34.0 %collective-permute-start.1 = (f32[1,16,128]{2,1,0:T(8,128)S(1)}, f32[1,16,128]{2,1,0:T(8,128)S(1)}, u32[]{:S(2)}, u32[]{:S(2)}) collective-permute-start(f32[1,16,128]{2,1,0:T(8,128)S(1)} %slice_bitcast_fusion.5), channel_id=1, source_target_pairs={{12,0},{0,4},{4,8},{8,12},{13,1},{1,5},{5,9},{9,13},{14,2},{2,6},{... | collective-permute-start | bytes 24584 | tf_op jit(solution)/shard_map/ppermute | solution.py:20
  5.5 34.5 %collective-permute-start.4 = (f32[16,1,128]{2,1,0:T(1,128)S(1)}, f32[16,1,128]{2,1,0:T(1,128)S(1)}, u32[]{:S(2)}, u32[]{:S(2)}) collective-permute-start(f32[16,1,128]{2,1,0:T(1,128)S(1)} %slice.228), channel_id=1, source_target_pairs={{0,2},{1,3},{4,6},{5,7},{8,10},{9,11},{12,14},{13,15},{16,18},{17,... | collective-permute-start | bytes 24584 | tf_op jit(solution)/shard_map/ppermute | solution.py:26
  8.9 0.7 copy-start.11
  20.5 0.7 copy-start.19
  26.3 4.3 %copy-start.2 = (f32[1,3,16,16,128]{4,3,2,1,0:T(8,128)S(1)}, f32[1,3,16,16,128]{4,3,2,1,0:T(8,128)}, u32[]{:S(2)}) copy-start(f32[1,3,16,16,128]{4,3,2,1,0:T(8,128)} %param.12) | copy-start | bytes 1179652
  26.3 7.3 %collective-permute-start.6 = (f32[5,32]{1,0:T(8,128)S(1)}, f32[5,32]{1,0:T(8,128)S(1)}, u32[]{:S(2)}, u32[]{:S(2)}) collective-permute-start(f32[5,32]{1,0:T(8,128)S(1)} %psum.43), channel_id=1, source_target_pairs={{0,1},{1,0},{2,3},{3,2},{4,5},{5,4},{6,7},{7,6},{8,9},{9,8},{10,11... | collective-permute-start | bytes 1928 | tf_op jit(solution)/shard_map/ppermute | solution.py:14
  26.7 13.4 %collective-permute-start.2 = (f32[5,1,16,128]{3,0,2,1:T(8,128)S(1)}, f32[5,1,16,128]{3,0,2,1:T(8,128)S(1)}, u32[]{:S(2)}, u32[]{:S(2)}) collective-permute-start(f32[5,1,16,128]{3,0,2,1:T(8,128)S(1)} %get-tuple-element.27), channel_id=1, source_target_pairs={{0,4},{4,8},{8,12},{12,0},{1,5},{5,9},{9,13},{13,1},{2,6},{6,10},{... | collective-permute-start | bytes 122888 | tf_op jit(solution)/shard_map/ppermute | solution.py:36
  26.8 14.5 %collective-permute-start = (f32[5,1,16,128]{3,0,2,1:T(8,128)S(1)}, f32[5,1,16,128]{3,0,2,1:T(8,128)S(1)}, u32[]{:S(2)}, u32[]{:S(2)}) collective-permute-start(f32[5,1,16,128]{3,0,2,1:T(8,128)S(1)} %get-tuple-element.26), channel_id=1, source_target_pairs={{4,0},{8,4},{12,8},{0,12},{5,1},{9,5},{13,9},{1,13},{6,2},{10,6},{... | collective-permute-start | bytes 122888 | tf_op jit(solution)/shard_map/ppermute | solution.py:37
  30.6 1.7 copy-start.13
  30.7 1.7 copy-start.20
  30.7 4.3 %copy-start.18 = (f32[1,5,5]{2,0,1:T(1,128)S(1)}, f32[1,5,5]{2,0,1:T(1,128)}, u32[]{:S(2)}) copy-start(f32[1,5,5]{2,0,1:T(1,128)} %param.17) | copy-start | bytes 304
  32.4 7.6 %copy-start.6 = (f32[1,16,16,128]{3,2,1,0:T(8,128)S(1)}, f32[1,16,16,128]{3,2,1,0:T(8,128)}, u32[]{:S(2)}) copy-start(f32[1,16,16,128]{3,2,1,0:T(8,128)} %param.13) | copy-start | bytes 393220
  33.6 8.8 %collective-permute-start.3 = (f32[5,16,1,128]{3,0,2,1:T(8,128)S(1)}, f32[5,16,1,128]{3,0,2,1:T(8,128)S(1)}, u32[]{:S(2)}, u32[]{:S(2)}) collective-permute-start(f32[5,16,1,128]{3,0,2,1:T(8,128)S(1)} %get-tuple-element.25), channel_id=1, source_target_pairs={{2,0},{3,1},{6,4},{7,5},{10,8},{11,9},{14,12},{15,13},{18,16},{19,... | collective-permute-start | bytes 122888 | tf_op jit(solution)/shard_map/ppermute | solution.py:37
  35.4 8.2 %collective-permute-start.5 = (f32[5,16,1,128]{3,0,2,1:T(8,128)S(1)}, f32[5,16,1,128]{3,0,2,1:T(8,128)S(1)}, u32[]{:S(2)}, u32[]{:S(2)}) collective-permute-start(f32[5,16,1,128]{3,0,2,1:T(8,128)S(1)} %get-tuple-element.24), channel_id=1, source_target_pairs={{0,2},{1,3},{4,6},{5,7},{8,10},{9,11},{12,14},{13,15},{16,18},{17,... | collective-permute-start | bytes 122888 | tf_op jit(solution)/shard_map/ppermute | solution.py:36
  40.1 6.3 %copy-start.7 = (f32[16,16,128]{2,1,0:T(8,128)}, f32[16,16,128]{2,1,0:T(8,128)S(1)}, u32[]{:S(2)}) copy-start(f32[16,16,128]{2,1,0:T(8,128)S(1)} %get-tuple-element.8) | copy-start | bytes 393220
  40.1 6.3 %copy-start.9 = (f32[16,16,128]{2,1,0:T(8,128)}, f32[16,16,128]{2,1,0:T(8,128)S(1)}, u32[]{:S(2)}) copy-start(f32[16,16,128]{2,1,0:T(8,128)S(1)} %get-tuple-element.31) | copy-start | bytes 393220
  43.6 1.2 copy-start.1
  44.8 1.5 copy-start.3
  44.8 1.6 copy-start.15
  64.3 9.7 %collective-permute-start.11 = (f32[5,32]{1,0:T(8,128)S(1)}, f32[5,32]{1,0:T(8,128)S(1)}, u32[]{:S(2)}, u32[]{:S(2)}) collective-permute-start(f32[5,32]{1,0:T(8,128)S(1)} %psum.45), channel_id=1, source_target_pairs={{0,1},{1,0},{2,3},{3,2},{4,5},{5,4},{6,7},{7,6},{8,9},{9,8},{10,11... | collective-permute-start | bytes 1928 | tf_op jit(solution)/shard_map/ppermute | solution.py:14
  64.3 10.2 %collective-permute-start.8 = (f32[5,1,16,128]{3,0,2,1:T(8,128)S(1)}, f32[5,1,16,128]{3,0,2,1:T(8,128)S(1)}, u32[]{:S(2)}, u32[]{:S(2)}) collective-permute-start(f32[5,1,16,128]{3,0,2,1:T(8,128)S(1)} %get-tuple-element.21), channel_id=1, source_target_pairs={{0,4},{4,8},{8,12},{12,0},{1,5},{5,9},{9,13},{13,1},{2,6},{6,10},{... | collective-permute-start | bytes 122888 | tf_op jit(solution)/shard_map/ppermute | solution.py:36
  66.2 9.4 %collective-permute-start.7 = (f32[5,1,16,128]{3,0,2,1:T(8,128)S(1)}, f32[5,1,16,128]{3,0,2,1:T(8,128)S(1)}, u32[]{:S(2)}, u32[]{:S(2)}) collective-permute-start(f32[5,1,16,128]{3,0,2,1:T(8,128)S(1)} %get-tuple-element.20), channel_id=1, source_target_pairs={{4,0},{8,4},{12,8},{0,12},{5,1},{9,5},{13,9},{1,13},{6,2},{10,6},{... | collective-permute-start | bytes 122888 | tf_op jit(solution)/shard_map/ppermute | solution.py:37
  68.2 8.6 %collective-permute-start.9 = (f32[5,16,1,128]{3,0,2,1:T(8,128)S(1)}, f32[5,16,1,128]{3,0,2,1:T(8,128)S(1)}, u32[]{:S(2)}, u32[]{:S(2)}) collective-permute-start(f32[5,16,1,128]{3,0,2,1:T(8,128)S(1)} %get-tuple-element.19), channel_id=1, source_target_pairs={{2,0},{3,1},{6,4},{7,5},{10,8},{11,9},{14,12},{15,13},{18,16},{19,... | collective-permute-start | bytes 122888 | tf_op jit(solution)/shard_map/ppermute | solution.py:37
  69.4 8.5 %collective-permute-start.10 = (f32[5,16,1,128]{3,0,2,1:T(8,128)S(1)}, f32[5,16,1,128]{3,0,2,1:T(8,128)S(1)}, u32[]{:S(2)}, u32[]{:S(2)}) collective-permute-start(f32[5,16,1,128]{3,0,2,1:T(8,128)S(1)} %get-tuple-element.18), channel_id=1, source_target_pairs={{0,2},{1,3},{4,6},{5,7},{8,10},{9,11},{12,14},{13,15},{16,18},{17,... | collective-permute-start | bytes 122888 | tf_op jit(solution)/shard_map/ppermute | solution.py:36
  79.1 1.2 copy-start.5
  79.1 1.2 copy-start.8
  79.1 1.2 copy-start.10
  79.1 1.5 copy-start.16
  98.5 10.5 %collective-permute-start.16 = (f32[5,32]{1,0:T(8,128)S(1)}, f32[5,32]{1,0:T(8,128)S(1)}, u32[]{:S(2)}, u32[]{:S(2)}) collective-permute-start(f32[5,32]{1,0:T(8,128)S(1)} %psum.47), channel_id=1, source_target_pairs={{0,1},{1,0},{2,3},{3,2},{4,5},{5,4},{6,7},{7,6},{8,9},{9,8},{10,11... | collective-permute-start | bytes 1928 | tf_op jit(solution)/shard_map/ppermute | solution.py:14
  99.2 10.4 %collective-permute-start.13 = (f32[5,1,16,128]{3,0,2,1:T(8,128)}, f32[5,1,16,128]{3,0,2,1:T(8,128)S(1)}, u32[]{:S(2)}, u32[]{:S(2)}) collective-permute-start(f32[5,1,16,128]{3,0,2,1:T(8,128)} %get-tuple-element.15), channel_id=1, source_target_pairs={{0,4},{4,8},{8,12},{12,0},{1,5},{5,9},{9,13},{13,1},{2,6},{6,10},{... | collective-permute-start | bytes 122888 | tf_op jit(solution)/shard_map/ppermute | solution.py:36
  100.9 9.8 %collective-permute-start.12 = (f32[5,1,16,128]{3,0,2,1:T(8,128)S(1)}, f32[5,1,16,128]{3,0,2,1:T(8,128)S(1)}, u32[]{:S(2)}, u32[]{:S(2)}) collective-permute-start(f32[5,1,16,128]{3,0,2,1:T(8,128)S(1)} %get-tuple-element.14), channel_id=1, source_target_pairs={{4,0},{8,4},{12,8},{0,12},{5,1},{9,5},{13,9},{1,13},{6,2},{10,6},{... | collective-permute-start | bytes 122888 | tf_op jit(solution)/shard_map/ppermute | solution.py:37
  103.0 8.8 %collective-permute-start.14 = (f32[5,16,1,128]{3,0,2,1:T(8,128)}, f32[5,16,1,128]{3,0,2,1:T(8,128)S(1)}, u32[]{:S(2)}, u32[]{:S(2)}) collective-permute-start(f32[5,16,1,128]{3,0,2,1:T(8,128)} %get-tuple-element.13), channel_id=1, source_target_pairs={{2,0},{3,1},{6,4},{7,5},{10,8},{11,9},{14,12},{15,13},{18,16},{19,... | collective-permute-start | bytes 122888 | tf_op jit(solution)/shard_map/ppermute | solution.py:37
  104.3 8.7 %collective-permute-start.15 = (f32[5,16,1,128]{3,0,2,1:T(8,128)S(1)}, f32[5,16,1,128]{3,0,2,1:T(8,128)S(1)}, u32[]{:S(2)}, u32[]{:S(2)}) collective-permute-start(f32[5,16,1,128]{3,0,2,1:T(8,128)S(1)} %get-tuple-element.12), channel_id=1, source_target_pairs={{0,2},{1,3},{4,6},{5,7},{8,10},{9,11},{12,14},{13,15},{16,18},{17,... | collective-permute-start | bytes 122888 | tf_op jit(solution)/shard_map/ppermute | solution.py:36
  114.1 1.2 copy-start.4
  114.2 1.4 copy-start.17
  117.4 1.0 copy-start.12
  118.4 0.7 copy-start.14
where the time goes:
time: 178 us; the launch traced here: 177 us
  blocking collectives  101 us (57%)
  starting transfers between devices  35.7 us (20%)
  matrix products  25.2 us (14%)
  local copies, waits for them, and re-layouts  12.6 us (7%)
  between operations  1.99 us (1%)
    unnamed x1, blocking collectives  57.6 us
    psum x3, blocking collectives, local(): face_sum = lax.psum(face_sum, 'theta')  28.2 us
    dot_general x18, matrix products, apply_block(): jnp.einsum('gf,gtra->ftra', matrix, values, precision=lax.Precision.HIGHEST)  24 us
    ppermute x6, starting transfers between devices, extended(): before = lax.ppermute(last, axis, up)  17.6 us
    psum x3, blocking collectives, local(): matched = lax.psum(matched, 'band')  14.8 us
    ppermute x6, starting transfers between devices, extended(): after = lax.ppermute(first, axis, down)  11.7 us
    unnamed x47, local copies, waits for them, and re-layouts  4.63 us
    slice x3, local copies, waits for them, and re-layouts, lower_shift(): lax.slice_in_dim(values, 0, values.shape[axis] - 1, axis=axis)  4.32 us
  transfers between devices with their start and end apart: 17, of which 0 were waited for; matrix products, arithmetic and copies ran while one was open for 10% of the time, Pallas kernels for 0%

commit v1 on v0

v1 whole, which is shorter than its diff:
```python
import functools

import jax
import jax.numpy as jnp
from jax import lax
from jax.experimental import pallas as pl
from jax.experimental.pallas import tpu as pltpu
from jax.sharding import PartitionSpec as P

ITERS = 3
OMEGA = 0.8
MESH = pl.DeviceIdType.MESH
F32 = jnp.float32
STEP = 2


def add_block(totals, jac, direction, side, values, sign=1.0):
    fields = len(values)
    for f in range(fields):
        for g in range(fields):
            term = jac[0, direction, side, g, f] * values[g]
            totals[f] = totals[f] + term if sign > 0 else totals[f] - term
    return totals


def kernel(
    sizes,
    adjoint,
    grad_hbm,
    coef_hbm,
    source_hbm,
    jac,
    weights,
    row_map,
    mix_jac,
    surf,
    modes,
    out,
    sens_out,
    field,
    coef,
    grad,
    scale,
    acc,
    theta_in,
    band_in,
    band_out,
    coef_theta,
    coef_band,
    coef_top,
    face_weight,
    one_hot,
    corr,
    plane,
    mix_out,
    mix_in,
    sens_part,
    sens_in,
    load_sem,
    send_sem,
    recv_sem,
    coef_send,
    coef_recv,
    mix_send,
    mix_recv,
    sens_send,
    sens_recv,
):
    n_theta, n_band, nf, nt, nr, na, own_modes = sizes
    group = n_theta * n_band * 2
    theta = lax.axis_index("theta")
    band = lax.axis_index("band")
    row = lax.axis_index("row")
    me = (theta * n_band + band) * 2 + row
    next_theta = lax.rem(theta + 1, n_theta)
    prev_theta = lax.rem(theta + n_theta - 1, n_theta)
    has_above = band < n_band - 1
    has_below = band > 0
    face = jnp.where(row == 0, na - 1, 0)

    def device(index):
        return {
            "theta": index // (2 * n_band),
            "band": lax.rem(index // 2, n_band),
            "row": lax.rem(index, 2),
        }

    def remote(src, dst, send, recv, **where):
        return pltpu.make_async_remote_copy(
            src_ref=src, dst_ref=dst, send_sem=send, recv_sem=recv,
            device_id=where, device_id_type=MESH,
        )

    loads = [
        pltpu.make_async_copy(adjoint.at[0], field.at[0, :, pl.ds(1, nt)], load_sem.at[0]),
        pltpu.make_async_copy(coef_hbm.at[0], coef.at[:, pl.ds(1, nt)], load_sem.at[1]),
        pltpu.make_async_copy(grad_hbm.at[0], grad, load_sem.at[2]),
        pltpu.make_async_copy(source_hbm.at[0], scale, load_sem.at[3]),
    ]
    for load in loads:
        load.start()

    barrier = pltpu.get_barrier_semaphore()

    def greet(i, carry):
        pl.semaphore_signal(
            barrier, inc=1, device_id=device(lax.rem(me + i, group)), device_id_type=MESH
        )
        return carry

    lax.fori_loop(1, group, greet, 0)

    layer = jnp.zeros((nr, na), F32)
    for k in range(ITERS):
        for f in range(nf):
            field[k, f, 0] = layer
            field[k, f, nt + 1] = layer
    coef[0, 0] = layer

    @pl.when(jnp.logical_not(has_above))
    def _():
        for k in range(ITERS):
            band_in[k, 1] = jnp.zeros((nf, nt, na), F32)

    @pl.when(jnp.logical_not(has_below))
    def _():
        for k in range(ITERS):
            band_in[k, 0] = jnp.zeros((nf, nt, na), F32)
        coef_band[...] = jnp.zeros((nt, na), F32)

    lanes = lax.broadcasted_iota(jnp.int32, (nr, na), 1)
    rows = lax.broadcasted_iota(jnp.int32, (nr, na), 0)
    at_face = lanes == face
    row_lanes = lax.broadcasted_iota(jnp.int32, (1, na), 1)
    eye = lax.broadcasted_iota(jnp.int32, (nr, nr), 0) == lax.broadcasted_iota(
        jnp.int32, (nr, nr), 1
    )
    for q in range(nr):
        one_hot[pl.ds(q, 1), :] = jnp.where(row_lanes == row_map[0, q], 1.0, 0.0)
    for t in range(nt):
        line = jnp.broadcast_to(weights[0, pl.ds(t, 1), :], (nr, nr))
        column = jnp.sum(jnp.where(eye, line, 0.0), axis=1, keepdims=True)
        face_weight[t] = jnp.where(at_face, column, 0.0)

    loads[0].wait()
    loads[1].wait()

    def pack(t, sums):
        result = []
        for f in range(nf):
            value = field[0, f, t + 1]
            band_out[0, 0, f, pl.ds(t, 1), :] = value[:1]
            band_out[0, 1, f, pl.ds(t, 1), :] = value[nr - 1 :]
            result.append(sums[f] + face_weight[t] * value)
        coef_top[pl.ds(t, 1), :] = coef[1, t + 1, pl.ds(nr - 1, 1), :]
        return tuple(result)

    def halo_copies(k):
        theta_copies = [
            remote(field.at[k, :, nt], theta_in.at[k, 0], send_sem.at[k, 0],
                   recv_sem.at[k, 0], theta=next_theta),
            remote(field.at[k, :, 1], theta_in.at[k, 1], send_sem.at[k, 1],
                   recv_sem.at[k, 1], theta=prev_theta),
        ]
        up = remote(band_out.at[k, 1], band_in.at[k, 0], send_sem.at[k, 2],
                    recv_sem.at[k, 2], band=band + 1)
        down = remote(band_out.at[k, 0], band_in.at[k, 1], send_sem.at[k, 3],
                      recv_sem.at[k, 3], band=band - 1)
        return theta_copies, up, down

    def mix_copies(k, start):
        slot = theta * n_band + band

        def one(i, carry):
            to = lax.rem(slot + i, n_theta * n_band)
            remote(mix_out.at[k], mix_in.at[k, slot], mix_send.at[k], mix_recv.at[k],
                   theta=to // n_band, band=lax.rem(to, n_band), row=1 - row).start()
            return carry

        lax.fori_loop(0, n_theta * n_band, one, 0)

    def send_mix(k, sums):
        hot = one_hot[...]
        for f in range(nf):
            column = jnp.sum(sums[f], axis=1, keepdims=True)
            mix_out[k, pl.ds(f, 1), :] = jnp.sum(hot * column, axis=0, keepdims=True)
        mix_copies(k, True)

    def start_halos(k):
        theta_copies, up, down = halo_copies(k)
        pl.when(has_above)(up.start)
        pl.when(has_below)(down.start)
        for copy in theta_copies:
            copy.start()

    zero_sums = tuple(jnp.zeros((nr, na), F32) for _ in range(nf))
    for k in range(ITERS):
        mix_out[k] = jnp.zeros((8, na), F32)
    sums = lax.fori_loop(0, nt, pack, zero_sums)

    pl.semaphore_wait(barrier, group - 1)
    coef_up = remote(coef_top, coef_band, coef_send.at[1], coef_recv.at[1], band=band + 1)
    coef_next = remote(coef.at[0, nt], coef_theta, coef_send.at[0], coef_recv.at[0],
                       theta=next_theta)
    send_mix(0, sums)
    start_halos(0)
    coef_next.start()
    pl.when(has_above)(coef_up.start)
    loads[2].wait()
    loads[3].wait()

    chunk_lanes = lax.broadcasted_iota(jnp.int32, (STEP, nr, na), 2)
    chunk_rows = lax.broadcasted_iota(jnp.int32, (STEP, nr, na), 1)

    def lane_up(v):
        return jnp.where(chunk_lanes == na - 1, 0.0, pltpu.roll(v, na - 1, 2))

    def lane_down(v):
        return jnp.where(chunk_lanes == 0, 0.0, pltpu.roll(v, 1, 2))

    def row_up(v):
        return jnp.where(chunk_rows == nr - 1, 0.0, pltpu.roll(v, nr - 1, 1))

    def row_down(v):
        return jnp.where(chunk_rows == 0, 0.0, pltpu.roll(v, 1, 1))

    for k in range(ITERS):

        def bulk(i, carry):
            t = i * STEP
            own = pl.ds(t + 1, STEP)
            total = [-grad[f, pl.ds(t, STEP)] for f in range(nf)]
            c_axial = coef[2, own]
            w = []
            for f in range(nf):
                v = field[k, f, own]
                w.append(c_axial * (v - lane_up(v)))
            total = add_block(total, jac, 2, 0, w)
            total = add_block(total, jac, 2, 1, [lane_down(x) for x in w])
            c_radial = coef[1, own]
            w = []
            for f in range(nf):
                v = field[k, f, own]
                w.append(c_radial * (v - row_up(v)))
            total = add_block(total, jac, 1, 0, w)
            total = add_block(total, jac, 1, 1, [row_down(x) for x in w])
            c_theta = coef[0, pl.ds(t, STEP + 1)]
            w = []
            for f in range(nf):
                v = field[k, f, pl.ds(t, STEP + 2)]
                w.append(c_theta * (v[: STEP + 1] - v[1:]))
            total = add_block(total, jac, 0, 0, [x[1:] for x in w])
            total = add_block(total, jac, 0, 1, [x[:STEP] for x in w])
            for f in range(nf):
                acc[f, pl.ds(t, STEP)] = total[f]
            if k == 0:
                low = row_down(c_radial) + lane_down(c_axial)
                scale[pl.ds(t, STEP)] = (
                    scale[pl.ds(t, STEP)] + c_theta[1:] + c_theta[:STEP] + c_radial + c_axial + low
                )
            return carry

        lax.fori_loop(0, nt // STEP, bulk, 0)

        theta_copies, up, down = halo_copies(k)
        for copy in theta_copies:
            copy.wait()
        if k == 0:
            coef_next.wait()

            @pl.when(has_above)
            def _():
                coef_up.wait_send()

            @pl.when(has_below)
            def _():
                coef_up.wait_recv()

            scale[0] += coef_theta[...]
        before = [coef_theta[...] * (theta_in[k, 0, f] - field[k, f, 1]) for f in range(nf)]
        total = add_block([acc[f, 0] for f in range(nf)], jac, 0, 1, before)
        for f in range(nf):
            acc[f, 0] = total[f]
        after = [coef[0, nt] * theta_in[k, 1, f] for f in range(nf)]
        total = add_block([acc[f, nt - 1] for f in range(nf)], jac, 0, 0, after, -1.0)
        for f in range(nf):
            acc[f, nt - 1] = total[f]

        @pl.when(has_above)
        def _():
            up.wait_send()
            down.wait_recv()

        @pl.when(has_below)
        def _():
            down.wait_send()
            up.wait_recv()

        flat = jnp.zeros((nt, na), F32)
        below = [coef_band[...] * (band_in[k, 0, f] - band_out[k, 0, f]) for f in range(nf)]
        total = add_block([flat] * nf, jac, 1, 1, below)
        above = [coef_top[...] * band_in[k, 1, f] for f in range(nf)]
        other = add_block([flat] * nf, jac, 1, 0, above, -1.0)
        for f in range(nf):
            corr[0, f] = total[f]
            corr[1, f] = other[f]

        pltpu.make_async_copy(mix_in.at[k], mix_in.at[k], mix_recv.at[k]).wait()
        pltpu.make_async_copy(mix_in.at[k], mix_in.at[k], mix_send.at[k]).wait()
        matched = lax.fori_loop(
            1, n_theta * n_band, lambda i, m: m + mix_in[k, i], mix_in[k, 0]
        )
        here = lanes == rows + band * nr
        for f in range(nf):
            line = mix_jac[0, 0, f] * matched[:1]
            for g in range(1, nf):
                line = line + mix_jac[0, g, f] * matched[g : g + 1]
            column = jnp.sum(jnp.where(here, line, 0.0), axis=1, keepdims=True)
            plane[f] = jnp.where(at_face, column, 0.0)

        def finish(t, sums):
            if k == 0:
                bottom = jnp.where(rows == 0, coef_band[pl.ds(t, 1), :], 0.0)
                gain = OMEGA / (scale[t] + bottom)
                scale[t] = gain
            else:
                gain = scale[t]
            result = []
            for f in range(nf):
                resid = acc[f, t] + plane[f]
                resid = resid + jnp.where(rows == 0, corr[0, f, pl.ds(t, 1), :], 0.0)
                resid = resid + jnp.where(rows == nr - 1, corr[1, f, pl.ds(t, 1), :], 0.0)
                value = field[k, f, t + 1] - gain * resid
                if k < ITERS - 1:
                    field[k + 1, f, t + 1] = value
                    band_out[k + 1, 0, f, pl.ds(t, 1), :] = value[:1]
                    band_out[k + 1, 1, f, pl.ds(t, 1), :] = value[nr - 1 :]
                    result.append(sums[f] + face_weight[t] * value)
                else:
                    out[0, f, t] = value
            return tuple(result) if k < ITERS - 1 else sums

        if k < ITERS - 1:
            sums = lax.fori_loop(0, nt, finish, zero_sums)
            send_mix(k + 1, sums)
            start_halos(k + 1)
        else:
            finish(0, 0)
            weighted = surf[0, 0, 0] * out[0, 0, 0]
            for f in range(1, nf):
                weighted = weighted + surf[0, f, 0] * out[0, f, 0]
            tile_rows = lax.broadcasted_iota(jnp.int32, (8, na), 0)

            def part(d, carry):
                mode = jnp.where(tile_rows < own_modes, tile_rows + d * own_modes, -1)
                total = jnp.zeros((8, na), F32)
                for r in range(nr):
                    total = total + jnp.where(mode == modes[0, 0, r], weighted[r : r + 1], 0.0)
                sens_part[d] = total
                return carry

            lax.fori_loop(0, group, part, 0)

            def send(i, carry):
                to = lax.rem(me + i, group)
                remote(sens_part.at[to], sens_in.at[i - 1], sens_send.at[0], sens_recv.at[0],
                       **device(to)).start()
                return carry

            lax.fori_loop(1, group, send, 0)
            lax.fori_loop(1, nt, finish, 0)
            pltpu.make_async_copy(sens_in, sens_in, sens_recv.at[0]).wait()
            pltpu.make_async_copy(sens_in, sens_in, sens_send.at[0]).wait()
            total = lax.fori_loop(0, group - 1, lambda i, s: s + sens_in[i], sens_part[me])
            sens_out[...] = total[:own_modes]


def local(sizes, *args):
    adjoint = args[0]
    n_theta, n_band, own_modes = sizes
    _, nf, nt, nr, na = adjoint.shape
    group = n_theta * n_band * 2
    dma = pltpu.SemaphoreType.DMA
    any_space = pl.BlockSpec(memory_space=pl.ANY)
    vmem = pl.BlockSpec(memory_space=pltpu.VMEM)
    smem = pl.BlockSpec(memory_space=pltpu.SMEM)
    return pl.pallas_call(
        functools.partial(kernel, (n_theta, n_band, nf, nt, nr, na, own_modes)),
        out_shape=(
            jax.ShapeDtypeStruct(adjoint.shape, F32),
            jax.ShapeDtypeStruct((own_modes, na), F32),
        ),
        in_specs=[any_space] * 4 + [smem, vmem, smem, smem, vmem, smem],
        out_specs=(vmem, vmem),
        scratch_shapes=[
            pltpu.VMEM((ITERS, nf, nt + 2, nr, na), F32),
            pltpu.VMEM((3, nt + 1, nr, na), F32),
            pltpu.VMEM((nf, nt, nr, na), F32),
            pltpu.VMEM((nt, nr, na), F32),
            pltpu.VMEM((nf, nt, nr, na), F32),
            pltpu.VMEM((ITERS, 2, nf, nr, na), F32),
            pltpu.VMEM((ITERS, 2, nf, nt, na), F32),
            pltpu.VMEM((ITERS, 2, nf, nt, na), F32),
            pltpu.VMEM((nr, na), F32),
            pltpu.VMEM((nt, na), F32),
            pltpu.VMEM((nt, na), F32),
            pltpu.VMEM((nt, nr, na), F32),
            pltpu.VMEM((nr, na), F32),
            pltpu.VMEM((2, nf, nt, na), F32),
            pltpu.VMEM((nf, nr, na), F32),
            pltpu.VMEM((ITERS, 8, na), F32),
            pltpu.VMEM((ITERS, n_theta * n_band, 8, na), F32),
            pltpu.VMEM((group, 8, na), F32),
            pltpu.VMEM((group - 1, 8, na), F32),
            dma((4,)),
            dma((ITERS, 4)),
            dma((ITERS, 4)),
            dma((2,)),
            dma((2,)),
            dma((ITERS,)),
            dma((ITERS,)),
            dma((1,)),
            dma((1,)),
        ],
        compiler_params=pltpu.CompilerParams(
            collective_id=0, has_side_effects=True, vmem_limit_bytes=40 * 1024 * 1024
        ),
    )(*args)


def solution(mesh):
    cells = P(("samples", "row"), None, "theta", "band", None)
    placed = (
        cells,
        cells,
        cells,
        P(("samples", "row"), "theta", "band", None),
        P("row", None, None, None, None),
        P(("samples", "row"), "theta", "band"),
        P(("samples", "row"), "band"),
        P("row", None, None),
        cells,
        P(("samples", "row"), "theta", "band"),
    )
    return jax.shard_map(
        functools.partial(local, (mesh.shape["theta"], mesh.shape["band"], 2)),
        mesh=mesh,
        in_specs=placed,
        out_specs=(cells, P(("samples", "theta", "band", "row"), None)),
        check_vma=False,
    )
```

time: 178 us -> 36.8 us (0.21)
  blocking collectives: 101 us -> 0 us
  starting transfers between devices: 35.7 us -> 0 us
  Pallas kernels: 0 us -> 28.1 us
  matrix products: 25.2 us -> 0 us
  local copies, waits for them, and re-layouts: 12.6 us -> 7.62 us
    unnamed x1 -> x0, blocking collectives: 57.6 us -> none
    psum x6 -> x0, blocking collectives: 43 us -> none  [the longest x3 28.2 us: local(): face_sum = lax.psum(face_sum, 'theta')]
    ppermute x17 -> x0, starting transfers between devices: 35.7 us -> none  [the longest x6 17.6 us: extended(): before = lax.ppermute(last, axis, up)]
    pallas_call x0 -> x1, Pallas kernels: none -> 28.1 us  [local(): pl.pallas_call(functools.partial(kernel, (n_theta, n_band, nf, nt, nr, na...]
    dot_general x25 -> x0, matrix products: 25.2 us -> none  [the longest x18 24 us: apply_block(): jnp.einsum('gf,gtra->ftra', matrix, values, precision=lax.Precision.HIGHEST)]
    slice x12 -> x0, local copies, waits for them, and re-layouts: 6.41 us -> none  [the longest x3 4.32 us: lower_shift(): lax.slice_in_dim(values, 0, values.shape[axis] - 1, axis=axis)]
    unnamed x47 -> x20, local copies, waits for them, and re-layouts: 4.63 us -> 7.62 us
  transfers between devices with their start and end apart: 17 -> 0, of which waited for: 0 -> 0; matrix products, arithmetic and copies ran while one was open for 10% -> 0% of each run, Pallas kernels for 0% -> 0%
where the time goes in v1:
time: 36.8 us; the launch traced here: 36.4 us
  Pallas kernels  28.1 us (76%)
  local copies, waits for them, and re-layouts  7.62 us (21%)
  between operations  0.67 us (2%)
    pallas_call x1, Pallas kernels, local(): pl.pallas_call(functools.partial(kernel, (n_theta, n_band, nf, nt, nr, na...  28.1 us
    unnamed x20, local copies, waits for them, and re-layouts  7.62 us

profile of v1, /device:TPU:0, one launch (start us, length us, event | category | flops | bytes accessed | tf_op | source)
XLA Modules:
  0.0 36.4 jit_solution(15781666261932608065)
XLA Ops:
  0.6 0.0 copy-start.4
  0.6 0.7 %copy.13.mix_jac = f32[1,5,5]{2,1,0:T(8,128)S(1)} copy(f32[1,5,5]{2,0,1:T(1,128)} %param.17) | data formatting | bytes 200 | tf_op args[7]
  1.3 0.0 copy-start.6
  1.3 0.0 copy-start.7
  1.3 0.7 %copy.12.jac = f32[1,3,2,5,5]{4,3,2,1,0:T(8,128)S(1)} copy(f32[1,3,2,5,5]{4,2,3,1,0:T(2,128)} %param.14) | data formatting | bytes 1200 | tf_op args[4]
  2.1 0.0 copy-done.4
  2.1 0.0 copy-done.6
  2.1 0.0 copy-done.7
  2.1 0.0 copy-start
  2.1 1.1 %copy-done = f32[1,5,16,16,128]{4,3,2,1,0:T(8,128)S(1)} copy-done((f32[1,5,16,16,128]{4,3,2,1,0:T(8,128)S(1)}, f32[1,5,16,16,128]{4,3,2,1,0:T(8,128)}, u32[]{:S(2)}) %copy-start) | copy-done | bytes 655384
  3.2 0.0 copy-start.1
  3.2 1.1 %copy-done.1 = f32[1,5,16,16,128]{4,3,2,1,0:T(8,128)S(1)} copy-done((f32[1,5,16,16,128]{4,3,2,1,0:T(8,128)S(1)}, f32[1,5,16,16,128]{4,3,2,1,0:T(8,128)}, u32[]{:S(2)}) %copy-start.1) | copy-done | bytes 655384
  4.3 0.0 copy-start.2
  4.3 1.0 %copy-done.2 = f32[1,3,16,16,128]{4,3,2,1,0:T(8,128)S(1)} copy-done((f32[1,3,16,16,128]{4,3,2,1,0:T(8,128)S(1)}, f32[1,3,16,16,128]{4,3,2,1,0:T(8,128)}, u32[]{:S(2)}) %copy-start.2) | copy-done | bytes 393240
  5.3 0.0 copy-start.3
  5.3 0.9 %copy-done.3 = f32[1,16,16,128]{3,2,1,0:T(8,128)S(1)} copy-done((f32[1,16,16,128]{3,2,1,0:T(8,128)S(1)}, f32[1,16,16,128]{3,2,1,0:T(8,128)}, u32[]{:S(2)}) %copy-start.3) | copy-done | bytes 131096
  6.2 0.0 copy-start.5
  6.2 0.7 %copy-done.5 = f32[1,16,16]{2,1,0:T(8,128)S(1)} copy-done((f32[1,16,16]{2,1,0:T(8,128)S(1)}, f32[1,16,16]{2,1,0:T(8,128)}, u32[]{:S(2)}) %copy-start.5) | copy-done | bytes 1048
  6.9 28.1 %shard_map.113 = (f32[1,5,16,16,128]{4,3,2,1,0:T(8,128)S(1)}, f32[2,128]{1,0:T(2,128)S(1)}) custom-call(f32[1,5,16,16,128]{4,3,2,1,0:T(8,128)S(1)} %copy-done, f32[1,5,16,16,128]{4,3,2,1,0:T(8,128)S(1)} %copy-done.1, f32[1,3,16,16,128]{4,3,2,1,0:T(8,128)S(1)} %copy-done.2, f32[1,16,16,128]{3,2,1,0:T(8,128)S(1)} %copy-done.3, ...), custom_call_target="tpu_custom_call" | custom-call | tf_op jit(solution)/shard_map/pallas_call | solution.py:387
  35.0 0.8 %copy.16 = f32[1,5,16,16,128]{4,3,2,1,0:T(8,128)} copy(f32[1,5,16,16,128]{4,3,2,1,0:T(8,128)S(1)} %get-tuple-element.4) | data formatting | bytes 1310720
  35.9 0.6 %copy.17 = f32[2,128]{1,0:T(2,128)} copy(f32[2,128]{1,0:T(2,128)S(1)} %get-tuple-element.5) | data formatting | bytes 2048
Async XLA Ops:
  0.6 1.5 %copy-start.4 = (f32[1,5,1,16,128]{4,3,2,1,0:T(8,128)S(1)}, f32[1,5,1,16,128]{4,3,2,1,0:T(8,128)}, u32[]{:S(2)}) copy-start(f32[1,5,1,16,128]{4,3,2,1,0:T(8,128)} %surf.1) | copy-start | bytes 122884
  1.3 0.8 %copy-start.6 = (s32[1,16]{1,0:T(1,128)S(1)}, s32[1,16]{1,0:T(1,128)}, u32[]{:S(2)}) copy-start(s32[1,16]{1,0:T(1,128)} %row_map.1) | copy-start | bytes 196
  1.3 0.8 %copy-start.7 = (s32[1,1,16]{2,1,0:T(1,128)S(1)}, s32[1,1,16]{2,1,0:T(1,128)}, u32[]{:S(2)}) copy-start(s32[1,1,16]{2,1,0:T(1,128)} %modes.1) | copy-start | bytes 196
  2.1 1.1 %copy-start = (f32[1,5,16,16,128]{4,3,2,1,0:T(8,128)S(1)}, f32[1,5,16,16,128]{4,3,2,1,0:T(8,128)}, u32[]{:S(2)}) copy-start(f32[1,5,16,16,128]{4,3,2,1,0:T(8,128)} %adjoint.1) | copy-start | bytes 1966084
  3.2 1.1 %copy-start.1 = (f32[1,5,16,16,128]{4,3,2,1,0:T(8,128)S(1)}, f32[1,5,16,16,128]{4,3,2,1,0:T(8,128)}, u32[]{:S(2)}) copy-start(f32[1,5,16,16,128]{4,3,2,1,0:T(8,128)} %grad_hbm.1) | copy-start | bytes 1966084
  4.3 1.0 %copy-start.2 = (f32[1,3,16,16,128]{4,3,2,1,0:T(8,128)S(1)}, f32[1,3,16,16,128]{4,3,2,1,0:T(8,128)}, u32[]{:S(2)}) copy-start(f32[1,3,16,16,128]{4,3,2,1,0:T(8,128)} %coef_hbm.1) | copy-start | bytes 1179652
  5.3 0.9 %copy-start.3 = (f32[1,16,16,128]{3,2,1,0:T(8,128)S(1)}, f32[1,16,16,128]{3,2,1,0:T(8,128)}, u32[]{:S(2)}) copy-start(f32[1,16,16,128]{3,2,1,0:T(8,128)} %source_hbm.1) | copy-start | bytes 393220
  6.2 0.7 %copy-start.5 = (f32[1,16,16]{2,1,0:T(8,128)S(1)}, f32[1,16,16]{2,1,0:T(8,128)}, u32[]{:S(2)}) copy-start(f32[1,16,16]{2,1,0:T(8,128)} %weights.1) | copy-start | bytes 3076

commit v2 on v1

--- a/solution.py
+++ b/solution.py
@@ -18,7 +18,7 @@
     fields = len(values)
     for f in range(fields):
         for g in range(fields):
-            term = jac[0, direction, side, g, f] * values[g]
+            term = jac[0, direction, g, side, f] * values[g]
             totals[f] = totals[f] + term if sign > 0 else totals[f] - term
     return totals
 
@@ -30,10 +30,10 @@
     coef_hbm,
     source_hbm,
     jac,
-    weights,
+    weights_hbm,
     row_map,
     mix_jac,
-    surf,
+    surf_hbm,
     modes,
     out,
     sens_out,
@@ -56,6 +56,8 @@
     mix_in,
     sens_part,
     sens_in,
+    weights,
+    surf,
     load_sem,
     send_sem,
     recv_sem,
@@ -96,6 +98,8 @@
         pltpu.make_async_copy(coef_hbm.at[0], coef.at[:, pl.ds(1, nt)], load_sem.at[1]),
         pltpu.make_async_copy(grad_hbm.at[0], grad, load_sem.at[2]),
         pltpu.make_async_copy(source_hbm.at[0], scale, load_sem.at[3]),
+        pltpu.make_async_copy(weights_hbm, weights, load_sem.at[4]),
+        pltpu.make_async_copy(surf_hbm, surf, load_sem.at[5]),
     ]
     for load in loads:
         load.start()
@@ -137,6 +141,7 @@
     )
     for q in range(nr):
         one_hot[pl.ds(q, 1), :] = jnp.where(row_lanes == row_map[0, q], 1.0, 0.0)
+    loads[4].wait()
     for t in range(nt):
         line = jnp.broadcast_to(weights[0, pl.ds(t, 1), :], (nr, nr))
         column = jnp.sum(jnp.where(eye, line, 0.0), axis=1, keepdims=True)
@@ -186,28 +191,31 @@
             mix_out[k, pl.ds(f, 1), :] = jnp.sum(hot * column, axis=0, keepdims=True)
         mix_copies(k, True)
 
-    def start_halos(k):
-        theta_copies, up, down = halo_copies(k)
+    def start_theta(k):
+        for copy in halo_copies(k)[0]:
+            copy.start()
+
+    def start_band(k):
+        _, up, down = halo_copies(k)
         pl.when(has_above)(up.start)
         pl.when(has_below)(down.start)
-        for copy in theta_copies:
-            copy.start()
 
     zero_sums = tuple(jnp.zeros((nr, na), F32) for _ in range(nf))
     for k in range(ITERS):
         mix_out[k] = jnp.zeros((8, na), F32)
-    sums = lax.fori_loop(0, nt, pack, zero_sums)
-
     pl.semaphore_wait(barrier, group - 1)
     coef_up = remote(coef_top, coef_band, coef_send.at[1], coef_recv.at[1], band=band + 1)
     coef_next = remote(coef.at[0, nt], coef_theta, coef_send.at[0], coef_recv.at[0],
                        theta=next_theta)
+    start_theta(0)
+    coef_next.start()
+    sums = lax.fori_loop(0, nt, pack, zero_sums)
     send_mix(0, sums)
-    start_halos(0)
-    coef_next.start()
+    start_band(0)
     pl.when(has_above)(coef_up.start)
     loads[2].wait()
     loads[3].wait()
+    loads[5].wait()
 
     chunk_lanes = lax.broadcasted_iota(jnp.int32, (STEP, nr, na), 2)
     chunk_rows = lax.broadcasted_iota(jnp.int32, (STEP, nr, na), 1)
@@ -263,48 +271,6 @@
         lax.fori_loop(0, nt // STEP, bulk, 0)
 
         theta_copies, up, down = halo_copies(k)
-        for copy in theta_copies:
-            copy.wait()
-        if k == 0:
-            coef_next.wait()
-
-            @pl.when(has_above)
-            def _():
-                coef_up.wait_send()
-
-            @pl.when(has_below)
-            def _():
-                coef_up.wait_recv()
-
-            scale[0] += coef_theta[...]
-        before = [coef_theta[...] * (theta_in[k, 0, f] - field[k, f, 1]) for f in range(nf)]
-        total = add_block([acc[f, 0] for f in range(nf)], jac, 0, 1, before)
-        for f in range(nf):
-            acc[f, 0] = total[f]
-        after = [coef[0, nt] * theta_in[k, 1, f] for f in range(nf)]
-        total = add_block([acc[f, nt - 1] for f in range(nf)], jac, 0, 0, after, -1.0)
-        for f in range(nf):
-            acc[f, nt - 1] = total[f]
-
-        @pl.when(has_above)
-        def _():
-            up.wait_send()
-            down.wait_recv()
-
-        @pl.when(has_below)
-        def _():
-            down.wait_send()
-            up.wait_recv()
-
-        flat = jnp.zeros((nt, na), F32)
-        below = [coef_band[...] * (band_in[k, 0, f] - band_out[k, 0, f]) for f in range(nf)]
-        total = add_block([flat] * nf, jac, 1, 1, below)
-        above = [coef_top[...] * band_in[k, 1, f] for f in range(nf)]
-        other = add_block([flat] * nf, jac, 1, 0, above, -1.0)
-        for f in range(nf):
-            corr[0, f] = total[f]
-            corr[1, f] = other[f]
-
         pltpu.make_async_copy(mix_in.at[k], mix_in.at[k], mix_recv.at[k]).wait()
         pltpu.make_async_copy(mix_in.at[k], mix_in.at[k], mix_send.at[k]).wait()
         matched = lax.fori_loop(
@@ -314,9 +280,53 @@
         for f in range(nf):
             line = mix_jac[0, 0, f] * matched[:1]
             for g in range(1, nf):
-                line = line + mix_jac[0, g, f] * matched[g : g + 1]
+                line = line + mix_jac[g, 0, f] * matched[g : g + 1]
             column = jnp.sum(jnp.where(here, line, 0.0), axis=1, keepdims=True)
             plane[f] = jnp.where(at_face, column, 0.0)
+
+        @pl.when(has_above)
+        def _():
+            up.wait_send()
+            down.wait_recv()
+
+        @pl.when(has_below)
+        def _():
+            down.wait_send()
+            up.wait_recv()
+
+        if k == 0:
+
+            @pl.when(has_above)
+            def _():
+                coef_up.wait_send()
+
+            @pl.when(has_below)
+            def _():
+                coef_up.wait_recv()
+
+        flat = jnp.zeros((nt, na), F32)
+        below = [coef_band[...] * (band_in[k, 0, f] - band_out[k, 0, f]) for f in range(nf)]
+        total = add_block([flat] * nf, jac, 1, 1, below)
+        above = [coef_top[...] * band_in[k, 1, f] for f in range(nf)]
+        other = add_block([flat] * nf, jac, 1, 0, above, -1.0)
+        for f in range(nf):
+            corr[0, f] = total[f]
+            corr[1, f] = other[f]
+
+        for copy in theta_copies:
+            copy.wait()
+        if k == 0:
+            coef_next.wait()
+
+            scale[0] += coef_theta[...]
+        before = [coef_theta[...] * (theta_in[k, 0, f] - field[k, f, 1]) for f in range(nf)]
+        total = add_block([acc[f, 0] for f in range(nf)], jac, 0, 1, before)
+        for f in range(nf):
+            acc[f, 0] = total[f]
+        after = [coef[0, nt] * theta_in[k, 1, f] for f in range(nf)]
+        total = add_block([acc[f, nt - 1] for f in range(nf)], jac, 0, 0, after, -1.0)
+        for f in range(nf):
+            acc[f, nt - 1] = total[f]
 
         def finish(t, sums):
             if k == 0:
@@ -343,7 +353,8 @@
         if k < ITERS - 1:
             sums = lax.fori_loop(0, nt, finish, zero_sums)
             send_mix(k + 1, sums)
-            start_halos(k + 1)
+            start_band(k + 1)
+            start_theta(k + 1)
         else:
             finish(0, 0)
             weighted = surf[0, 0, 0] * out[0, 0, 0]
@@ -351,15 +362,18 @@
                 weighted = weighted + surf[0, f, 0] * out[0, f, 0]
             tile_rows = lax.broadcasted_iota(jnp.int32, (8, na), 0)
 
+            owners = 8 // own_modes
+
             def part(d, carry):
-                mode = jnp.where(tile_rows < own_modes, tile_rows + d * own_modes, -1)
+                mode = tile_rows + d * 8
                 total = jnp.zeros((8, na), F32)
                 for r in range(nr):
                     total = total + jnp.where(mode == modes[0, 0, r], weighted[r : r + 1], 0.0)
-                sens_part[d] = total
+                for j in range(owners):
+                    sens_part[d * owners + j] = total[j * own_modes : (j + 1) * own_modes]
                 return carry
 
-            lax.fori_loop(0, group, part, 0)
+            lax.fori_loop(0, group // owners, part, 0)
 
             def send(i, carry):
                 to = lax.rem(me + i, group)
@@ -372,7 +386,7 @@
             pltpu.make_async_copy(sens_in, sens_in, sens_recv.at[0]).wait()
             pltpu.make_async_copy(sens_in, sens_in, sens_send.at[0]).wait()
             total = lax.fori_loop(0, group - 1, lambda i, s: s + sens_in[i], sens_part[me])
-            sens_out[...] = total[:own_modes]
+            sens_out[...] = total
 
 
 def local(sizes, *args):
@@ -381,16 +395,16 @@
     _, nf, nt, nr, na = adjoint.shape
     group = n_theta * n_band * 2
     dma = pltpu.SemaphoreType.DMA
-    any_space = pl.BlockSpec(memory_space=pl.ANY)
+    hbm = pl.BlockSpec(memory_space=pltpu.HBM)
     vmem = pl.BlockSpec(memory_space=pltpu.VMEM)
     smem = pl.BlockSpec(memory_space=pltpu.SMEM)
     return pl.pallas_call(
         functools.partial(kernel, (n_theta, n_band, nf, nt, nr, na, own_modes)),
         out_shape=(
-            jax.ShapeDtypeStruct(adjoint.shape, F32),
-            jax.ShapeDtypeStruct((own_modes, na), F32),
+            pltpu.VMEM(adjoint.shape, F32),
+            pltpu.VMEM((own_modes, na), F32),
         ),
-        in_specs=[any_space] * 4 + [smem, vmem, smem, smem, vmem, smem],
+        in_specs=[hbm] * 4 + [smem, hbm, smem, smem, hbm, smem],
         out_specs=(vmem, vmem),
         scratch_shapes=[
             pltpu.VMEM((ITERS, nf, nt + 2, nr, na), F32),
@@ -410,9 +424,11 @@
             pltpu.VMEM((nf, nr, na), F32),
             pltpu.VMEM((ITERS, 8, na), F32),
             pltpu.VMEM((ITERS, n_theta * n_band, 8, na), F32),
-            pltpu.VMEM((group, 8, na), F32),
-            pltpu.VMEM((group - 1, 8, na), F32),
-            dma((4,)),
+            pltpu.VMEM((group, own_modes, na), F32),
+            pltpu.VMEM((group - 1, own_modes, na), F32),
+            pltpu.VMEM((1, nt, nr), F32),
+            pltpu.VMEM((1, nf, 1, nr, na), F32),
+            dma((6,)),
             dma((ITERS, 4)),
             dma((ITERS, 4)),
             dma((2,)),
@@ -423,9 +439,9 @@
             dma((1,)),
         ],
         compiler_params=pltpu.CompilerParams(
-            collective_id=0, has_side_effects=True, vmem_limit_bytes=40 * 1024 * 1024
+            collective_id=0, has_side_effects=True, vmem_limit_bytes=63 * 1024 * 1024
         ),
-    )(*args)
+    )(*args[:4], jnp.swapaxes(args[4], 2, 3), *args[5:7], jnp.swapaxes(args[7], 0, 1), *args[8:])
 
 
 def solution(mesh):

time: 36.8 us -> 29.8 us (0.81)
  local copies, waits for them, and re-layouts: 7.62 us -> 1.4 us
  Pallas kernels: 28.1 us -> 27.5 us
    unnamed x20 -> x2, local copies, waits for them, and re-layouts: 7.62 us -> 1.4 us
    pallas_call x1, Pallas kernels: 28.1 us -> 27.5 us  [local(): pl.pallas_call(functools.partial(kernel, (n_theta, n_band, nf, nt, nr, na...]
where the time goes in v2:
time: 29.8 us; the launch traced here: 29.6 us
  Pallas kernels  27.5 us (92%)
  local copies, waits for them, and re-layouts  1.4 us (5%)
  between operations  0.64 us (2%)
    pallas_call x1, Pallas kernels, local(): pl.pallas_call(functools.partial(kernel, (n_theta, n_band, nf, nt, nr, na...  27.5 us
    unnamed x2, local copies, waits for them, and re-layouts  1.4 us

profile of v2, /device:TPU:0, one launch (start us, length us, event | category | flops | bytes accessed | tf_op | source)
XLA Modules:
  0.0 29.6 jit_solution(10223604288248959555)
XLA Ops:
  0.6 27.5 %shard_map.113 = (f32[1,5,16,16,128]{4,3,2,1,0:T(8,128)S(1)}, f32[2,128]{1,0:T(2,128)S(1)}) custom-call(f32[1,5,16,16,128]{4,3,2,1,0:T(8,128)} %adjoint.1, f32[1,5,16,16,128]{4,3,2,1,0:T(8,128)} %grad_hbm.1, f32[1,3,16,16,128]{4,3,2,1,0:T(8,128)} %coef_hbm.1, f32[1,16,16,128]{3,2,1,0:T(8,128)} %source_hbm.1, f32[1,3,5,2,5]{4,3,2,1,0:T(2,128)} %bitcast.2, ...), custom_call_target="tpu_custom_call" | custom-call | tf_op jit(solution)/shard_map/pallas_call | solution.py:401
  28.2 0.8 %copy.14 = f32[1,5,16,16,128]{4,3,2,1,0:T(8,128)} copy(f32[1,5,16,16,128]{4,3,2,1,0:T(8,128)S(1)} %get-tuple-element.2) | data formatting | bytes 1310720
  29.0 0.6 %copy.15 = f32[2,128]{1,0:T(2,128)} copy(f32[2,128]{1,0:T(2,128)S(1)} %get-tuple-element.3) | data formatting | bytes 2048

commit v3 on v2

--- a/solution.py
+++ b/solution.py
@@ -177,7 +177,7 @@
         slot = theta * n_band + band
 
         def one(i, carry):
-            to = lax.rem(slot + i, n_theta * n_band)
+            to = lax.rem(slot + i + n_theta * n_band // 2, n_theta * n_band)
             remote(mix_out.at[k], mix_in.at[k, slot], mix_send.at[k], mix_recv.at[k],
                    theta=to // n_band, band=lax.rem(to, n_band), row=1 - row).start()
             return carry
@@ -192,8 +192,10 @@
         mix_copies(k, True)
 
     def start_theta(k):
-        for copy in halo_copies(k)[0]:
-            copy.start()
+        ahead, behind = halo_copies(k)[0]
+        pl.when(theta == 0)(behind.start)
+        ahead.start()
+        pl.when(theta > 0)(behind.start)
 
     def start_band(k):
         _, up, down = halo_copies(k)
@@ -207,11 +209,11 @@
     coef_up = remote(coef_top, coef_band, coef_send.at[1], coef_recv.at[1], band=band + 1)
     coef_next = remote(coef.at[0, nt], coef_theta, coef_send.at[0], coef_recv.at[0],
                        theta=next_theta)
+    sums = lax.fori_loop(0, nt, pack, zero_sums, unroll=4)
+    send_mix(0, sums)
     start_theta(0)
+    start_band(0)
     coef_next.start()
-    sums = lax.fori_loop(0, nt, pack, zero_sums)
-    send_mix(0, sums)
-    start_band(0)
     pl.when(has_above)(coef_up.start)
     loads[2].wait()
     loads[3].wait()
@@ -351,7 +353,7 @@
             return tuple(result) if k < ITERS - 1 else sums
 
         if k < ITERS - 1:
-            sums = lax.fori_loop(0, nt, finish, zero_sums)
+            sums = lax.fori_loop(0, nt, finish, zero_sums, unroll=4)
             send_mix(k + 1, sums)
             start_band(k + 1)
             start_theta(k + 1)
@@ -373,7 +375,7 @@
                     sens_part[d * owners + j] = total[j * own_modes : (j + 1) * own_modes]
                 return carry
 
-            lax.fori_loop(0, group // owners, part, 0)
+            lax.fori_loop(0, group // owners, part, 0, unroll=2)
 
             def send(i, carry):
                 to = lax.rem(me + i, group)
@@ -382,7 +384,7 @@
                 return carry
 
             lax.fori_loop(1, group, send, 0)
-            lax.fori_loop(1, nt, finish, 0)
+            lax.fori_loop(1, nt, finish, 0, unroll=3)
             pltpu.make_async_copy(sens_in, sens_in, sens_recv.at[0]).wait()
             pltpu.make_async_copy(sens_in, sens_in, sens_send.at[0]).wait()
             total = lax.fori_loop(0, group - 1, lambda i, s: s + sens_in[i], sens_part[me])

time: 29.8 us -> 28.2 us (0.946)
  Pallas kernels: 27.5 us -> 26 us
    pallas_call x1, Pallas kernels: 27.5 us -> 26 us  [local(): pl.pallas_call(functools.partial(kernel, (n_theta, n_band, nf, nt, nr, na...]
where the time goes in v3:
time: 28.2 us; the launch traced here: 28 us
  Pallas kernels  26 us (92%)
  local copies, waits for them, and re-layouts  1.4 us (5%)
  between operations  0.64 us (2%)
    pallas_call x1, Pallas kernels, local(): pl.pallas_call(functools.partial(kernel, (n_theta, n_band, nf, nt, nr, na...  26 us
    unnamed x2, local copies, waits for them, and re-layouts  1.4 us

profile of v3, /device:TPU:0, one launch (start us, length us, event | category | flops | bytes accessed | tf_op | source)
XLA Modules:
  0.0 28.0 jit_solution(13954561577781952906)
XLA Ops:
  0.6 26.0 %shard_map.113 = (f32[1,5,16,16,128]{4,3,2,1,0:T(8,128)S(1)}, f32[2,128]{1,0:T(2,128)S(1)}) custom-call(f32[1,5,16,16,128]{4,3,2,1,0:T(8,128)} %adjoint.1, f32[1,5,16,16,128]{4,3,2,1,0:T(8,128)} %grad_hbm.1, f32[1,3,16,16,128]{4,3,2,1,0:T(8,128)} %coef_hbm.1, f32[1,16,16,128]{3,2,1,0:T(8,128)} %source_hbm.1, f32[1,3,5,2,5]{4,3,2,1,0:T(2,128)} %bitcast.2, ...), custom_call_target="tpu_custom_call" | custom-call | tf_op jit(solution)/shard_map/pallas_call | solution.py:403
  26.6 0.8 %copy.14 = f32[1,5,16,16,128]{4,3,2,1,0:T(8,128)} copy(f32[1,5,16,16,128]{4,3,2,1,0:T(8,128)S(1)} %get-tuple-element.2) | data formatting | bytes 1310720
  27.5 0.6 %copy.15 = f32[2,128]{1,0:T(2,128)} copy(f32[2,128]{1,0:T(2,128)S(1)} %get-tuple-element.3) | data formatting | bytes 2048
